TPU v7x, 32 devices: a whole 2x2x4 slice. The times are simulated.
32 devices in a mesh: grp: 2 (over x), dap: 16 (over z, y, core), ch: 1.
Axes of the slice: x: 2, y: 2, z: 4, core: 2. Of those that a mesh axis runs over, the one named last changes fastest.
Arguments:
- pair: bfloat16 [256, 128, 128], P(('grp', 'dap')), parts along dimension 0, may hold values from -6 to 6
- cotangent: bfloat16 [256, 128, 128], P(('grp', 'dap')), parts along dimension 0, may hold values from -6 to 6
- pair_mask: int32 [256, 128], P(('grp', 'dap')), parts along dimension 0, may hold values 0 or 1
- w_a_gate: bfloat16 [128, 128], P(None, 'ch'), may hold values from -0.5 to 0.5
- w_a_proj: bfloat16 [128, 128], P(None, 'ch'), may hold values from -0.5 to 0.5
- w_b_gate: bfloat16 [128, 128], P(None, 'ch'), may hold values from -0.5 to 0.5
- w_b_proj: bfloat16 [128, 128], P(None, 'ch'), may hold values from -0.5 to 0.5
- w_gate: bfloat16 [128, 128], replicated, may hold values from -0.5 to 0.5
- w_out: bfloat16 [128, 128], P('ch'), may hold values from -0.5 to 0.5
Outputs:
- pair_grad: float32 [256, 128, 128], P(('grp', 'dap')), parts along dimension 0
There are 2 independent parts, one for each index of `grp`. A program takes and returns all parts, laid end to end along the dimension named above; an argument that names none is the same for every part. Nothing has to cross between parts.
All inputs are finite; a program needn't handle non-finite values. No bound on the sum of `pair_mask` on one device may be relied on, other than what follows from the above.
Results may differ from a plain program's by a relative error of at most 0.0068.
Values may be sent and summed in bfloat16 or wider, within the bound.
A program may use at most 128 MiB of HBM per device.

v0:
```python
import jax
import jax.numpy as jnp
from jax import lax
from jax.sharding import PartitionSpec as P


def matmul(left, right):
    return jnp.dot(left, right, preferred_element_type=jnp.float32)


def shards(pair, cotangent, pair_mask, w_a_gate, w_a_proj, w_b_gate, w_b_proj, w_gate, w_out):
    hidden_all = w_out.shape[0] * lax.axis_size("ch")
    pair_f = pair.astype(jnp.float32)
    mean_c = jnp.mean(pair_f, axis=-1, keepdims=True)
    inv_std = lax.rsqrt(jnp.mean(pair_f * pair_f, axis=-1, keepdims=True) - mean_c * mean_c + 1e-05)
    normed = (pair_f - mean_c) * inv_std
    normed_b = normed.astype(jnp.bfloat16)
    masked = pair_mask.astype(jnp.float32)[:, :, None]
    a_gate = jax.nn.sigmoid(matmul(normed_b, w_a_gate))
    a_proj = matmul(normed_b, w_a_proj)
    b_gate = jax.nn.sigmoid(matmul(normed_b, w_b_gate))
    b_proj = matmul(normed_b, w_b_proj)
    left = (a_gate * a_proj * masked).astype(jnp.bfloat16)
    right = (b_gate * b_proj * masked).astype(jnp.bfloat16)
    right_all = lax.all_gather(right, "dap", axis=0, tiled=True)
    tri = jnp.einsum("ikc,jkc->ijc", left, right_all, preferred_element_type=jnp.float32)
    sum_one, sum_two = lax.psum((jnp.sum(tri, axis=-1), jnp.sum(tri * tri, axis=-1)), "ch")
    mean_h = (sum_one / hidden_all)[:, :, None]
    inv_h = lax.rsqrt((sum_two / hidden_all)[:, :, None] - mean_h * mean_h + 1e-05)
    tri_n = (tri - mean_h) * inv_h
    update = lax.psum(matmul(tri_n.astype(jnp.bfloat16), w_out).astype(jnp.bfloat16), "ch").astype(
        jnp.float32
    )
    gate = jax.nn.sigmoid(matmul(normed_b, w_gate))
    cot_f = cotangent.astype(jnp.float32)
    d_upd = cot_f * gate
    d_gate_pre = cot_f * update * gate * (1.0 - gate)
    d_trin = matmul(d_upd.astype(jnp.bfloat16), w_out.T)
    grad_one, grad_two = lax.psum(
        (jnp.sum(d_trin, axis=-1), jnp.sum(d_trin * tri_n, axis=-1)), "ch"
    )
    d_tri = inv_h * (
        d_trin - (grad_one / hidden_all)[:, :, None] - tri_n * (grad_two / hidden_all)[:, :, None]
    )
    d_tri = d_tri.astype(jnp.bfloat16)
    d_left = jnp.einsum("ijc,jkc->ikc", d_tri, right_all, preferred_element_type=jnp.float32)
    d_right = lax.psum_scatter(
        jnp.einsum("ijc,ikc->jkc", d_tri, left, preferred_element_type=jnp.float32),
        "dap",
        scatter_dimension=0,
        tiled=True,
    )
    dla = (d_left * a_proj * masked * a_gate * (1.0 - a_gate)).astype(jnp.bfloat16)
    dlp = (d_left * a_gate * masked).astype(jnp.bfloat16)
    drb = (d_right * b_proj * masked * b_gate * (1.0 - b_gate)).astype(jnp.bfloat16)
    drp = (d_right * b_gate * masked).astype(jnp.bfloat16)
    partial_grad = (
        matmul(dla, w_a_gate.T)
        + matmul(dlp, w_a_proj.T)
        + matmul(drb, w_b_gate.T)
        + matmul(drp, w_b_proj.T)
    )
    d_normed = lax.psum(partial_grad, "ch") + matmul(d_gate_pre.astype(jnp.bfloat16), w_gate.T)
    return inv_std * (
        d_normed
        - jnp.mean(d_normed, axis=-1, keepdims=True)
        - normed * jnp.mean(d_normed * normed, axis=-1, keepdims=True)
    )


def solution(mesh):
    return jax.shard_map(
        shards,
        mesh=mesh,
        in_specs=(
            P(("grp", "dap"), None, None),
            P(("grp", "dap"), None, None),
            P(("grp", "dap"), None),
            P(None, "ch"),
            P(None, "ch"),
            P(None, "ch"),
            P(None, "ch"),
            P(),
            P("ch", None),
        ),
        out_specs=P(("grp", "dap"), None, None),
        check_vma=False,
    )
```

profile of v0, /device:TPU:0, one launch (start us, length us, event | category | flops | bytes accessed | tf_op | source)
XLA Modules:
  0.0 207.9 jit_solution(3371254999464820019)
XLA Ops:
  6.5 0.7 convert_element_type.50
  7.2 1.1 copy.25
  8.4 0.0 copy-start.8
  8.4 0.1 fusion.16
  8.5 1.1 fusion.8
  9.6 0.0 copy-start.4
  9.6 1.2 fusion.57
  10.8 0.3 fusion.52
  11.1 1.2 multiply_convert_fusion.3
  12.3 0.0 all-gather.2.cloned.1.call-update
  12.3 0.0 reduce-scatter.2.cloned.1.call-start
  12.4 0.2 copy.31
  12.6 0.3 fusion.2
  13.0 0.2 fusion.70
  13.2 52.5 %all-gather.2.cloned.1.call-done = bf16[128,128,128]{2,1,0:T(8,128)(2,1)} async-done(((bf16[8,128,128]{2,1,0:T(8,128)(2,1)}), bf16[128,128,128]{2,1,0:T(8,128)(2,1)}) %all-gather.2.cloned.1.call-update) | async-done | bytes 4194320 | tf_op jit(solution)/shard_map/all_gather | solution.py:25
  65.8 6.7 %copy.35 = bf16[128,128,128]{1,0,2:T(8,128)(2,1)} copy(bf16[128,128,128]{2,1,0:T(8,128)(2,1)} %all-gather.2.cloned.1.call-done) | data formatting | bytes 8388608 | tf_op jit(solution)/shard_map/all_gather | solution.py:25
  72.5 4.4 %multiply_reduce_fusion.1 = (f32[8,128]{1,0:T(8,128)S(1)}, f32[8,128]{1,0:T(8,128)S(1)}, f32[8,128,128]{1,0,2:T(8,128)S(1)}) fusion(bf16[128,128,128]{1,0,2:T(8,128)(2,1)} %copy.35, bf16[8,128,128]{1,0,2:T(8,128)(2,1)S(1)} %copy.31), kind=kOutput, calls=%fused_computation.51 | convolution fusion | flops 33945600 | bytes 4988928 | tf_op jit(solution)/shard_map/ikc,jkc->ijc/dot_general | solution.py:26
  77.0 1.0 fusion.31
  78.0 0.3 multiply_convert_fusion.2
  78.3 4.5 %fusion.76 = f32[128,128,128]{2,1,0:T(8,128)} fusion(bf16[8,128,128]{1,0,2:T(8,128)(2,1)S(1)} %copy.31, bf16[8,128,128]{1,0,2:T(8,128)(2,1)S(1)} %multiply_convert_fusion.2), kind=kOutput, calls=%fused_computation.93 | convolution fusion | flops 33554432 | bytes 8912896 | tf_op jit(solution)/shard_map/ijc,ikc->jkc/dot_general | solution.py:48
  82.8 9.4 %copy.38 = f32[128,128,128]{0,1,2:T(8,128)} copy(f32[128,128,128]{2,1,0:T(8,128)} %fusion.76) | data formatting | bytes 16777216 | tf_op jit(solution)/shard_map/ijc,ikc->jkc/dot_general | solution.py:48
  92.2 0.0 reduce-scatter.2.cloned.1.call-update
  92.2 3.4 %fusion.75 = f32[128,128,8]{1,2,0:T(8,128)S(1)} fusion(bf16[128,128,128]{1,0,2:T(8,128)(2,1)} %copy.35, bf16[8,128,128]{1,0,2:T(8,128)(2,1)S(1)} %multiply_convert_fusion.2), kind=kOutput, calls=%fused_computation.92 | convolution fusion | flops 33554432 | bytes 4980736 | tf_op jit(solution)/shard_map/ijc,jkc->ikc/dot_general | solution.py:46
  95.6 0.2 copy.36
  95.9 1.5 fusion.33
  97.4 1.5 convolution_add_fusion.3
  98.9 96.6 %reduce-scatter.2.cloned.1.call-done = f32[8,128,128]{2,1,0:T(8,128)} async-done(((f32[128,128,128]{2,1,0:T(8,128)}), f32[8,128,128]{2,1,0:T(8,128)}) %reduce-scatter.2.cloned.1.call-update) | async-done | bytes 524304 | tf_op jit(solution)/shard_map/reduce_scatter | solution.py:47
  195.5 1.4 convolution_add_fusion.2
  196.9 1.4 convolution_add_fusion.1
  198.3 1.5 fusion.69
  199.9 0.1 fusion.23
  200.0 1.0 copy.39
  (22 shorter events, 0.1 us)
Async XLA Ops:
  6.5 4.5 %copy-start = (bf16[128,128]{1,0:T(8,128)(2,1)S(1)}, bf16[128,128]{1,0:T(8,128)(2,1)}, u32[]{:S(2)}) copy-start(bf16[128,128]{1,0:T(8,128)(2,1)} %param.12) | copy-start | bytes 98308
  6.5 4.2 %copy-start.5 = (bf16[128,128]{1,0:T(8,128)(2,1)S(1)}, bf16[128,128]{1,0:T(8,128)(2,1)}, u32[]{:S(2)}) copy-start(bf16[128,128]{1,0:T(8,128)(2,1)} %param.13) | copy-start | bytes 98308
  6.5 59.2 %all-gather.2.cloned.1.call-start = ((), (), s32[]{:S(2)}) async-start(), calls=%async_computation.1 | async-start | bytes 4456448 | tf_op jit(solution)/shard_map/all_gather | solution.py:25
  8.4 4.2 %copy-start.8 = (bf16[128,128]{1,0:T(8,128)(2,1)S(1)}, bf16[128,128]{1,0:T(8,128)(2,1)}, u32[]{:S(2)}) copy-start(bf16[128,128]{1,0:T(8,128)(2,1)} %param.16) | copy-start | bytes 98308
  9.6 1.5 copy-start.1
  9.6 3.3 %copy-start.4 = (bf16[8,128,128]{2,1,0:T(8,128)(2,1)S(1)}, bf16[8,128,128]{2,1,0:T(8,128)(2,1)}, u32[]{:S(2)}) copy-start(bf16[8,128,128]{2,1,0:T(8,128)(2,1)} %param.10) | copy-start | bytes 786436
  9.6 3.3 %copy-start.7 = (bf16[128,128]{1,0:T(8,128)(2,1)S(1)}, bf16[128,128]{1,0:T(8,128)(2,1)}, u32[]{:S(2)}) copy-start(bf16[128,128]{1,0:T(8,128)(2,1)} %param.17) | copy-start | bytes 98308
  12.3 183.1 %reduce-scatter.2.cloned.1.call-start = ((), (), s32[]{:S(2)}) async-start(), calls=%async_computation.2 | async-start | bytes 8912896 | tf_op jit(solution)/shard_map/reduce_scatter | solution.py:47
  95.6 99.9 %copy-start.2 = (f32[8,128,128]{2,1,0:T(8,128)S(1)}, f32[8,128,128]{2,1,0:T(8,128)}, u32[]{:S(2)}) copy-start(f32[8,128,128]{2,1,0:T(8,128)} %copy-done.1) | copy-start | bytes 1572868
  95.6 101.3 %copy-start.6 = (bf16[128,128]{1,0:T(8,128)(2,1)S(1)}, bf16[128,128]{1,0:T(8,128)(2,1)}, u32[]{:S(2)}) copy-start(bf16[128,128]{1,0:T(8,128)(2,1)} %param.15) | copy-start | bytes 98308
  95.9 101.1 %copy-start.3 = (f32[8,128,128]{2,1,0:T(8,128)S(1)}, f32[8,128,128]{2,1,0:T(8,128)}, u32[]{:S(2)}) copy-start(f32[8,128,128]{2,1,0:T(8,128)} %copy-done.1) | copy-start | bytes 1572868
Sparse Core Ops, SparseCore 0:
  12.5 53.2 all-gather.1
  92.4 103.0 reduce-scatter.1
where the time goes:
time: 209 us; the launch traced here: 208 us
  waiting for transfers between devices  149 us (71%)
  matrix products  24 us (11%)
  local copies, waits for them, and re-layouts  18.7 us (9%)
  between operations  13.6 us (7%)
  other arithmetic  2.32 us (1%)
    reduce_scatter x1, waiting for transfers between devices, shards(): lax.psum_scatter(jnp.einsum('ijc,ikc->jkc', d_tri, left, preferred_elemen...  96.6 us
    all_gather x1, waiting for transfers between devices, shards(): right_all = lax.all_gather(right, 'dap', axis=0, tiled=True)  52.5 us
    dot_general x11, matrix products, matmul(): return jnp.dot(left, right, preferred_element_type=jnp.float32)  11.7 us
    dot_general x1, local copies, waits for them, and re-layouts, shards(): jnp.einsum('ijc,ikc->jkc', d_tri, left, preferred_element_type=jnp.float32)  9.36 us
    all_gather x1, local copies, waits for them, and re-layouts, shards(): right_all = lax.all_gather(right, 'dap', axis=0, tiled=True)  6.73 us
    dot_general x1, matrix products, shards(): jnp.einsum('ijc,ikc->jkc', d_tri, left, preferred_element_type=jnp.float32)  4.52 us
    dot_general x1, matrix products, shards(): jnp.einsum('ikc,jkc->ijc', left, right_all, preferred_element_type=jnp.fl...  4.44 us
  transfers between devices with their start and end apart: 2, of which 2 were waited for; matrix products, arithmetic and copies ran while one was open for 4% of the time, Pallas kernels for 0%

commit v1 on v0

--- a/solution.py
+++ b/solution.py
@@ -1,7 +1,14 @@
+import functools
+
 import jax
 import jax.numpy as jnp
 from jax import lax
+from jax.experimental import pallas as pl
+from jax.experimental.pallas import tpu as pltpu
 from jax.sharding import PartitionSpec as P
+
+F32, BF16 = jnp.float32, jnp.bfloat16
+ROWS = 8
 
 
 def matmul(left, right):
@@ -68,9 +75,234 @@
     )
 
 
+def transposed(w):
+    return w[...].astype(F32).T
+
+
+def interleaved(w_a, w_b, n):
+    width = w_a.shape[0]
+    both = jnp.concatenate(
+        [transposed(w_a).reshape(n, ROWS, width), transposed(w_b).reshape(n, ROWS, width)], axis=1
+    )
+    return both.reshape(2 * n * ROWS, width)
+
+
+def fused_kernel(
+    n, pair, cotangent, pair_mask, w_a_gate, w_a_proj, w_b_gate, w_b_proj, w_gate, w_out, out,
+    normed_s, inv_s, gate_s, proj_s, og_s, dtrin_s, dpre_s, pos_buf, both_s, tri_s, grad_s,
+    send1, recv1, send2, recv2, send3, recv3, send4, recv4, send_sem, recv_sem,
+):
+    me = lax.axis_index("dap")
+    chans = w_out.shape[0]
+    length = pair.shape[1]
+
+    def peer_of(off):
+        return lax.rem(me + off, n)
+
+    def source_of(off):
+        return lax.rem(me + n - off, n)
+
+    def copy_to(phase, send, recv, off):
+        peer = peer_of(off)
+        return pltpu.make_async_remote_copy(
+            src_ref=send.at[peer],
+            dst_ref=recv.at[me],
+            send_sem=send_sem.at[phase, off],
+            recv_sem=recv_sem.at[phase, off],
+            device_id={"dap": peer},
+            device_id_type=pl.DeviceIdType.MESH,
+        )
+
+    def exchange(phase, send, recv, block, unpack, meanwhile=None):
+        @pl.loop(1, n)
+        def _(off):
+            peer = peer_of(off)
+            send[peer] = block(peer).astype(BF16)
+            copy_to(phase, send, recv, off).start()
+
+        unpack(me, block(me).astype(BF16).astype(F32))
+        if meanwhile is not None:
+            meanwhile()
+
+        @pl.loop(1, n)
+        def _(off):
+            copy_to(phase, send, recv, off).wait_recv()
+            source = source_of(off)
+            unpack(source, recv[source].astype(F32))
+
+    barrier = pltpu.get_barrier_semaphore()
+
+    @pl.loop(1, n)
+    def _(off):
+        pl.semaphore_signal(
+            barrier, inc=1, device_id={"dap": peer_of(off)}, device_id_type=pl.DeviceIdType.MESH
+        )
+
+    gate_t = interleaved(w_a_gate, w_b_gate, n)
+    proj_t = interleaved(w_a_proj, w_b_proj, n)
+    gate_tb, proj_tb = gate_t.astype(BF16), proj_t.astype(BF16)
+    for i in range(ROWS):
+        x = pair[i].astype(F32).T
+        mu = jnp.mean(x, axis=0, keepdims=True)
+        inv = lax.rsqrt(jnp.mean(x * x, axis=0, keepdims=True) - mu * mu + 1e-05)
+        normed = (x - mu) * inv
+        normed_s[i] = normed
+        inv_s[i] = inv
+        normed_b = normed.astype(BF16)
+        gate = jax.nn.sigmoid(matmul(gate_tb, normed_b))
+        proj = matmul(proj_tb, normed_b)
+        gate_s[i] = gate
+        proj_s[i] = proj
+        masked = pair_mask[i : i + 1, :].astype(F32)
+        pos_buf[pl.ds(i, 2 * chans, stride=ROWS), :] = gate * proj * masked
+    pl.semaphore_wait(barrier, n - 1)
+
+    def rows_of(count):
+        size = count * ROWS
+        return lambda d: pos_buf[pl.ds(pl.multiple_of(d * size, size), size), :]
+
+    def to_channels(buf, count):
+        def unpack(s, values):
+            buf[:, pl.ds(pl.multiple_of(s * ROWS, ROWS), ROWS), :] = values.reshape(
+                count, ROWS, length
+            )
+
+        return unpack
+
+    def from_channels(buf, count):
+        return lambda d: buf[:, pl.ds(pl.multiple_of(d * ROWS, ROWS), ROWS), :].reshape(
+            count * ROWS, length
+        )
+
+    def to_rows(count):
+        size = count * ROWS
+
+        def unpack(s, values):
+            pos_buf[pl.ds(pl.multiple_of(s * size, size), size), :] = values
+
+        return unpack
+
+    def output_side():
+        og_t = transposed(w_gate).astype(BF16)
+        for i in range(ROWS):
+            gate = jax.nn.sigmoid(matmul(og_t, normed_s[i].astype(BF16)))
+            d_upd = cotangent[i].astype(F32).T * gate
+            dtrin_s[i] = matmul(w_out[...], d_upd.astype(BF16))
+            og_s[i] = d_upd * (1.0 - gate)
+
+    exchange(0, send1, recv1, rows_of(2 * ROWS), to_channels(both_s, 2 * ROWS), output_side)
+
+    for c in range(ROWS):
+        tri_s[c] = lax.dot_general(
+            both_s[c].astype(BF16),
+            both_s[ROWS + c].astype(BF16),
+            (((1,), (1,)), ((), ())),
+            preferred_element_type=F32,
+        )
+    exchange(1, send2, recv2, from_channels(tri_s, ROWS), to_rows(ROWS))
+
+    out_t = transposed(w_out).astype(BF16)
+    for i in range(ROWS):
+        rows = pl.ds(i, chans, stride=ROWS)
+        tri = pos_buf[rows, :]
+        mean_h = jnp.mean(tri, axis=0, keepdims=True)
+        inv_h = lax.rsqrt(jnp.mean(tri * tri, axis=0, keepdims=True) - mean_h * mean_h + 1e-05)
+        tri_n = (tri - mean_h) * inv_h
+        update = matmul(out_t, tri_n.astype(BF16))
+        dpre_s[i] = (og_s[i] * update).astype(BF16)
+        d_trin = dtrin_s[i]
+        one = jnp.mean(d_trin, axis=0, keepdims=True)
+        two = jnp.mean(d_trin * tri_n, axis=0, keepdims=True)
+        pos_buf[rows, :] = inv_h * (d_trin - one - tri_n * two)
+
+    exchange(2, send3, recv3, rows_of(ROWS), to_channels(tri_s, ROWS))
+
+    for c in range(ROWS):
+        d_tri = tri_s[c]
+        grad_s[c] = matmul(d_tri.astype(BF16), both_s[ROWS + c].astype(BF16))
+        grad_s[ROWS + c] = matmul(d_tri.T.astype(BF16), both_s[c].astype(BF16))
+
+    exchange(3, send4, recv4, from_channels(grad_s, 2 * ROWS), to_rows(2 * ROWS))
+
+    gate_w, proj_w = gate_t.T.astype(BF16), proj_t.T.astype(BF16)
+    for i in range(ROWS):
+        grad = pos_buf[pl.ds(i, 2 * chans, stride=ROWS), :] * pair_mask[i : i + 1, :].astype(F32)
+        gate = gate_s[i]
+        d_proj = grad * gate
+        d_gate = d_proj * proj_s[i] * (1.0 - gate)
+        d_normed = (
+            matmul(gate_w, d_gate.astype(BF16))
+            + matmul(proj_w, d_proj.astype(BF16))
+            + matmul(w_gate[...], dpre_s[i])
+        )
+        normed = normed_s[i]
+        out[i] = inv_s[i] * (
+            d_normed
+            - jnp.mean(d_normed, axis=0, keepdims=True)
+            - normed * jnp.mean(d_normed * normed, axis=0, keepdims=True)
+        )
+
+    for phase, send, recv in ((0, send1, recv1), (1, send2, recv2), (2, send3, recv3), (3, send4, recv4)):
+
+        @pl.loop(1, n)
+        def _(off):
+            copy_to(phase, send, recv, off).wait_send()
+
+
+def fused_shards(n, pair, *rest):
+    rows, length, chans = pair.shape
+    wide, narrow = 2 * ROWS * ROWS, ROWS * ROWS
+    grad_t = pl.pallas_call(
+        functools.partial(fused_kernel, n),
+        out_shape=jax.ShapeDtypeStruct((rows, chans, length), F32),
+        in_specs=[pl.BlockSpec(memory_space=pltpu.VMEM)] * 9,
+        out_specs=pl.BlockSpec(memory_space=pltpu.VMEM),
+        scratch_shapes=[
+            pltpu.VMEM((rows, chans, length), F32),
+            pltpu.VMEM((rows, 1, length), F32),
+            pltpu.VMEM((rows, 2 * chans, length), F32),
+            pltpu.VMEM((rows, 2 * chans, length), F32),
+            pltpu.VMEM((rows, chans, length), F32),
+            pltpu.VMEM((rows, chans, length), F32),
+            pltpu.VMEM((rows, chans, length), BF16),
+            pltpu.VMEM((2 * chans * rows, length), F32),
+            pltpu.VMEM((2 * ROWS, length, length), F32),
+            pltpu.VMEM((ROWS, length, length), F32),
+            pltpu.VMEM((2 * ROWS, length, length), F32),
+            pltpu.VMEM((n, wide, length), BF16),
+            pltpu.VMEM((n, wide, length), BF16),
+            pltpu.VMEM((n, narrow, length), BF16),
+            pltpu.VMEM((n, narrow, length), BF16),
+            pltpu.VMEM((n, narrow, length), BF16),
+            pltpu.VMEM((n, narrow, length), BF16),
+            pltpu.VMEM((n, wide, length), BF16),
+            pltpu.VMEM((n, wide, length), BF16),
+            pltpu.SemaphoreType.DMA((4, n)),
+            pltpu.SemaphoreType.DMA((4, n)),
+        ],
+        compiler_params=pltpu.CompilerParams(
+            collective_id=0, has_side_effects=True, vmem_limit_bytes=48 * 1024 * 1024
+        ),
+    )(pair, *rest)
+    return jnp.swapaxes(grad_t, 1, 2)
+
+
+def body_for(mesh):
+    n = mesh.shape["dap"]
+
+    def body(pair, *rest):
+        rows, length, chans = pair.shape
+        fits = mesh.shape["ch"] == 1 and n > 1 and rows == ROWS and chans == n * ROWS
+        if fits and length == rows * n == 128:
+            return fused_shards(n, pair, *rest)
+        return shards(pair, *rest)
+
+    return body
+
+
 def solution(mesh):
     return jax.shard_map(
-        shards,
+        body_for(mesh),
         mesh=mesh,
         in_specs=(
             P(("grp", "dap"), None, None),

time: 209 us -> 56.5 us (0.27)
  the two profiles are of different devices: /device:TPU:0 before, /device:TPU:25 now
where the time goes in v1:
time: 56.5 us; the launch traced here: 55.9 us
  Pallas kernels  47.8 us (85%)
  local copies, waits for them, and re-layouts  8.13 us (14%)
    pallas_call x1, Pallas kernels, fused_shards(): pl.pallas_call(functools.partial(fused_kernel, n), out_shape=jax.ShapeDty...  47.8 us
    unnamed x18, local copies, waits for them, and re-layouts  7.13 us

profile of v1, /device:TPU:25, one launch (start us, length us, event | category | flops | bytes accessed | tf_op | source)
XLA Modules:
  0.0 55.9 jit_solution(1798065519530736974)
XLA Ops:
  0.0 0.0 copy-start
  0.0 0.9 %copy-done = bf16[8,128,128]{2,1,0:T(8,128)(2,1)S(1)} copy-done((bf16[8,128,128]{2,1,0:T(8,128)(2,1)S(1)}, bf16[8,128,128]{2,1,0:T(8,128)(2,1)}, u32[]{:S(2)}) %copy-start) | copy-done | bytes 262168
  1.0 0.0 copy-start.1
  1.0 0.9 %copy-done.1 = bf16[8,128,128]{2,1,0:T(8,128)(2,1)S(1)} copy-done((bf16[8,128,128]{2,1,0:T(8,128)(2,1)S(1)}, bf16[8,128,128]{2,1,0:T(8,128)(2,1)}, u32[]{:S(2)}) %copy-start.1) | copy-done | bytes 262168
  1.9 0.0 copy-start.2
  1.9 0.8 %copy-done.2 = bf16[128,128]{1,0:T(8,128)(2,1)S(1)} copy-done((bf16[128,128]{1,0:T(8,128)(2,1)S(1)}, bf16[128,128]{1,0:T(8,128)(2,1)}, u32[]{:S(2)}) %copy-start.2) | copy-done | bytes 32792
  2.7 0.0 copy-start.3
  2.7 0.8 %copy-done.3 = bf16[128,128]{1,0:T(8,128)(2,1)S(1)} copy-done((bf16[128,128]{1,0:T(8,128)(2,1)S(1)}, bf16[128,128]{1,0:T(8,128)(2,1)}, u32[]{:S(2)}) %copy-start.3) | copy-done | bytes 32792
  3.4 0.0 copy-start.4
  3.4 0.8 %copy-done.4 = bf16[128,128]{1,0:T(8,128)(2,1)S(1)} copy-done((bf16[128,128]{1,0:T(8,128)(2,1)S(1)}, bf16[128,128]{1,0:T(8,128)(2,1)}, u32[]{:S(2)}) %copy-start.4) | copy-done | bytes 32792
  4.2 0.0 copy-start.5
  4.2 0.8 %copy-done.5 = bf16[128,128]{1,0:T(8,128)(2,1)S(1)} copy-done((bf16[128,128]{1,0:T(8,128)(2,1)S(1)}, bf16[128,128]{1,0:T(8,128)(2,1)}, u32[]{:S(2)}) %copy-start.5) | copy-done | bytes 32792
  4.9 0.0 copy-start.6
  4.9 0.8 %copy-done.6 = bf16[128,128]{1,0:T(8,128)(2,1)S(1)} copy-done((bf16[128,128]{1,0:T(8,128)(2,1)S(1)}, bf16[128,128]{1,0:T(8,128)(2,1)}, u32[]{:S(2)}) %copy-start.6) | copy-done | bytes 32792
  5.7 0.0 copy-start.7
  5.7 0.8 %copy-done.7 = bf16[128,128]{1,0:T(8,128)(2,1)S(1)} copy-done((bf16[128,128]{1,0:T(8,128)(2,1)S(1)}, bf16[128,128]{1,0:T(8,128)(2,1)}, u32[]{:S(2)}) %copy-start.7) | copy-done | bytes 32792
  6.5 0.0 copy-start.8
  6.5 0.7 %copy-done.8 = s32[8,128]{1,0:T(8,128)S(1)} copy-done((s32[8,128]{1,0:T(8,128)S(1)}, s32[8,128]{1,0:T(8,128)}, u32[]{:S(2)}) %copy-start.8) | copy-done | bytes 4120
  7.1 47.8 %shard_map.91 = f32[8,128,128]{2,1,0:T(8,128)S(1)} custom-call(bf16[8,128,128]{2,1,0:T(8,128)(2,1)S(1)} %copy-done, bf16[8,128,128]{2,1,0:T(8,128)(2,1)S(1)} %copy-done.1, s32[8,128]{1,0:T(8,128)S(1)} %copy-done.8, bf16[128,128]{1,0:T(8,128)(2,1)S(1)} %copy-done.2, bf16[128,128]{1,0:T(8,128)(2,1)S(1)} %copy-done.3, bf16[128,128]{1,0:T(8,128)(2,1)S(1)} %copy-done.4, ...), custom_call_target="tpu_custom_call" | custom-call | tf_op jit(solution)/shard_map/pallas_call | solution.py:255
  54.9 1.0 %copy.10 = f32[8,128,128]{2,1,0:T(8,128)} copy(f32[8,128,128]{1,2,0:T(8,128)S(1)} %bitcast.1) | data formatting | bytes 1048576 | tf_op jit(solution)/shard_map/transpose | solution.py:287
Async XLA Ops:
  0.0 0.9 %copy-start = (bf16[8,128,128]{2,1,0:T(8,128)(2,1)S(1)}, bf16[8,128,128]{2,1,0:T(8,128)(2,1)}, u32[]{:S(2)}) copy-start(bf16[8,128,128]{2,1,0:T(8,128)(2,1)} %pair.1) | copy-start | bytes 786436
  1.0 0.9 %copy-start.1 = (bf16[8,128,128]{2,1,0:T(8,128)(2,1)S(1)}, bf16[8,128,128]{2,1,0:T(8,128)(2,1)}, u32[]{:S(2)}) copy-start(bf16[8,128,128]{2,1,0:T(8,128)(2,1)} %cotangent.1) | copy-start | bytes 786436
  1.9 0.8 %copy-start.2 = (bf16[128,128]{1,0:T(8,128)(2,1)S(1)}, bf16[128,128]{1,0:T(8,128)(2,1)}, u32[]{:S(2)}) copy-start(bf16[128,128]{1,0:T(8,128)(2,1)} %w_a_gate.1) | copy-start | bytes 98308
  2.7 0.8 %copy-start.3 = (bf16[128,128]{1,0:T(8,128)(2,1)S(1)}, bf16[128,128]{1,0:T(8,128)(2,1)}, u32[]{:S(2)}) copy-start(bf16[128,128]{1,0:T(8,128)(2,1)} %w_a_proj.1) | copy-start | bytes 98308
  3.4 0.8 %copy-start.4 = (bf16[128,128]{1,0:T(8,128)(2,1)S(1)}, bf16[128,128]{1,0:T(8,128)(2,1)}, u32[]{:S(2)}) copy-start(bf16[128,128]{1,0:T(8,128)(2,1)} %w_b_gate.1) | copy-start | bytes 98308
  4.2 0.8 %copy-start.5 = (bf16[128,128]{1,0:T(8,128)(2,1)S(1)}, bf16[128,128]{1,0:T(8,128)(2,1)}, u32[]{:S(2)}) copy-start(bf16[128,128]{1,0:T(8,128)(2,1)} %w_b_proj.1) | copy-start | bytes 98308
  4.9 0.8 %copy-start.6 = (bf16[128,128]{1,0:T(8,128)(2,1)S(1)}, bf16[128,128]{1,0:T(8,128)(2,1)}, u32[]{:S(2)}) copy-start(bf16[128,128]{1,0:T(8,128)(2,1)} %w_gate.1) | copy-start | bytes 98308
  5.7 0.8 %copy-start.7 = (bf16[128,128]{1,0:T(8,128)(2,1)S(1)}, bf16[128,128]{1,0:T(8,128)(2,1)}, u32[]{:S(2)}) copy-start(bf16[128,128]{1,0:T(8,128)(2,1)} %w_out.1) | copy-start | bytes 98308
  6.5 0.7 %copy-start.8 = (s32[8,128]{1,0:T(8,128)S(1)}, s32[8,128]{1,0:T(8,128)}, u32[]{:S(2)}) copy-start(s32[8,128]{1,0:T(8,128)} %pair_mask.1) | copy-start | bytes 12292

commit v2 on v0

--- a/solution.py
+++ b/solution.py
@@ -1,7 +1,14 @@
+import functools
+
 import jax
 import jax.numpy as jnp
 from jax import lax
+from jax.experimental import pallas as pl
+from jax.experimental.pallas import tpu as pltpu
 from jax.sharding import PartitionSpec as P
+
+F32, BF16 = jnp.float32, jnp.bfloat16
+ROWS = 8
 
 
 def matmul(left, right):
@@ -68,9 +75,331 @@
     )
 
 
+def transposed(w):
+    return w[...].astype(F32).T
+
+
+def interleaved(w_a, w_b, parts):
+    chans, width = w_a.shape[1], w_a.shape[0]
+    shape = (parts, chans // parts, width)
+    both = jnp.concatenate([transposed(w_a).reshape(shape), transposed(w_b).reshape(shape)], axis=1)
+    return both.reshape(2 * chans, width)
+
+
+def fused_kernel(n, *refs):
+    inputs, out, held, refs = refs[:9], refs[9], refs[10:19], refs[19:]
+    (
+        normed_s, nb_s, inv_s, gate_s, proj_s, og_s, dtrin_s, dpre_s, pos_buf, left_s, right_s, tri_s,
+        dleft_s, dright_s, send1, recv1, far1, send2, recv2, send3, recv3, send4, recv4, sfar4, far4,
+        send_sem, recv_sem, in_sem,
+    ) = refs
+    pair, cotangent, pair_mask, w_a_gate, w_a_proj, w_b_gate, w_b_proj, w_gate, w_out = held
+    chans = w_out.shape[0]
+    length = pair.shape[1]
+    parts = n // 2
+    width = chans // parts
+    block = width * ROWS
+    me = lax.axis_index("dap")
+    mine = lax.rem(me, parts)
+    own_base = me - mine
+    far_base = parts - own_base
+
+    loads = [pltpu.make_async_copy(inputs[x], held[x], in_sem.at[x]) for x in range(9)]
+    for load in loads:
+        load.start()
+
+    barrier = pltpu.get_barrier_semaphore()
+
+    @pl.loop(1, n)
+    def _(off):
+        pl.semaphore_signal(
+            barrier,
+            inc=1,
+            device_id={"dap": lax.rem(me + off, n)},
+            device_id_type=pl.DeviceIdType.MESH,
+        )
+
+    def copy(phase, far, src, dst, to, source):
+        base, slot = (far_base, parts) if far else (own_base, 0)
+        return pltpu.make_async_remote_copy(
+            src_ref=src,
+            dst_ref=dst,
+            send_sem=send_sem.at[phase, slot + to],
+            recv_sem=recv_sem.at[phase, slot + source],
+            device_id={"dap": base + to},
+            device_id_type=pl.DeviceIdType.MESH,
+        )
+
+    def turn(t):
+        return lax.rem(mine + t, parts)
+
+    def at_rows(d):
+        return pl.ds(pl.multiple_of(d * ROWS, ROWS), ROWS)
+
+    def at_blocks(d, size):
+        return pl.ds(pl.multiple_of(d * size, size), size)
+
+    def grouped(values):
+        return values.reshape(values.shape[0] // ROWS, ROWS, length)
+
+    for load in loads:
+        load.wait()
+    gate_t = interleaved(w_a_gate, w_b_gate, parts)
+    proj_t = interleaved(w_a_proj, w_b_proj, parts)
+    gate_tb, proj_tb = gate_t.astype(BF16), proj_t.astype(BF16)
+    for i in range(ROWS):
+        x = pair[i].astype(F32).T
+        mu = jnp.mean(x, axis=0, keepdims=True)
+        inv = lax.rsqrt(jnp.mean(x * x, axis=0, keepdims=True) - mu * mu + 1e-05)
+        normed = (x - mu) * inv
+        normed_s[i] = normed
+        inv_s[i] = inv
+        nb_s[i] = normed.astype(BF16)
+
+    few = parts // 2
+    for g in range(2):
+        rows = slice(g * chans, (g + 1) * chans)
+        for i in range(ROWS):
+            gate = jax.nn.sigmoid(matmul(gate_tb[rows], nb_s[i]))
+            proj = matmul(proj_tb[rows], nb_s[i])
+            gate_s[i, rows] = gate
+            proj_s[i, rows] = proj
+            masked = pair_mask[i : i + 1, :].astype(F32)
+            pos_buf[pl.ds(g * chans * ROWS + i, chans, stride=ROWS), :] = gate * proj * masked
+        if g == 0:
+            pl.semaphore_wait(barrier, n - 1)
+
+        @pl.loop(0, few)
+        def _(t):
+            q = g * few + lax.rem(mine + t, few)
+            send1[q] = pos_buf[at_blocks(q, 2 * block), :].astype(BF16)
+            copy(0, True, send1.at[q, pl.ds(block, block)], far1.at[mine], q, mine).start()
+
+            @pl.when(q != mine)
+            def _():
+                copy(0, False, send1.at[q], recv1.at[mine], q, mine).start()
+
+    og_t = transposed(w_gate).astype(BF16)
+    for i in range(ROWS):
+        gate = jax.nn.sigmoid(matmul(og_t, nb_s[i]))
+        d_upd = cotangent[i].astype(F32).T * gate
+        dtrin_s[i] = matmul(w_out[...], d_upd.astype(BF16))
+        og_s[i] = d_upd * (1.0 - gate)
+
+    def keep(s, values):
+        values = grouped(values.astype(F32))
+        left_s[:, at_rows(s), :] = values[:width]
+        right_s[:, at_rows(own_base + s), :] = values[width:]
+
+    keep(mine, send1[mine])
+
+    @pl.loop(1, parts)
+    def _(t):
+        s = turn(t)
+        copy(0, False, send1.at[s], recv1.at[s], s, s).wait_recv()
+        keep(s, recv1[s])
+
+    @pl.loop(0, parts)
+    def _(t):
+        s = turn(t)
+        copy(0, True, send1.at[s, pl.ds(block, block)], far1.at[s], s, s).wait_recv()
+        right_s[:, at_rows(far_base + s), :] = grouped(far1[s].astype(F32))
+
+    for c in range(width):
+        tri_s[c] = lax.dot_general(
+            left_s[c].astype(BF16),
+            right_s[c].astype(BF16),
+            (((1,), (1,)), ((), ())),
+            preferred_element_type=F32,
+        )
+
+    def tri_block(q):
+        return tri_s[:, at_rows(q), :].reshape(block, length)
+
+    @pl.loop(1, parts)
+    def _(t):
+        q = turn(t)
+        send2[q] = tri_block(q).astype(BF16)
+        copy(1, False, send2.at[q], recv2.at[mine], q, mine).start()
+
+    pos_buf[at_blocks(mine, block), :] = tri_block(mine)
+
+    @pl.loop(1, parts)
+    def _(t):
+        s = turn(t)
+        copy(1, False, send2.at[s], recv2.at[s], s, s).wait_recv()
+        pos_buf[at_blocks(s, block), :] = recv2[s].astype(F32)
+
+    out_t = transposed(w_out).astype(BF16)
+    for i in range(ROWS):
+        rows = pl.ds(i, chans, stride=ROWS)
+        tri = pos_buf[rows, :]
+        mean_h = jnp.mean(tri, axis=0, keepdims=True)
+        inv_h = lax.rsqrt(jnp.mean(tri * tri, axis=0, keepdims=True) - mean_h * mean_h + 1e-05)
+        tri_n = (tri - mean_h) * inv_h
+        update = matmul(out_t, tri_n.astype(BF16))
+        dpre_s[i] = (og_s[i] * update).astype(BF16)
+        d_trin = dtrin_s[i]
+        one = jnp.mean(d_trin, axis=0, keepdims=True)
+        two = jnp.mean(d_trin * tri_n, axis=0, keepdims=True)
+        pos_buf[rows, :] = inv_h * (d_trin - one - tri_n * two)
+
+    @pl.loop(1, parts)
+    def _(t):
+        q = turn(t)
+        send3[q] = pos_buf[at_blocks(q, block), :].astype(BF16)
+        copy(2, False, send3.at[q], recv3.at[mine], q, mine).start()
+
+    tri_s[:, at_rows(mine), :] = grouped(pos_buf[at_blocks(mine, block), :])
+
+    @pl.loop(1, parts)
+    def _(t):
+        s = turn(t)
+        copy(2, False, send3.at[s], recv3.at[s], s, s).wait_recv()
+        tri_s[:, at_rows(s), :] = grouped(recv3[s].astype(F32))
+
+    for c in range(width):
+        dright_s[c] = matmul(tri_s[c].T.astype(BF16), left_s[c].astype(BF16))
+
+    @pl.loop(0, parts)
+    def _(t):
+        q = turn(t)
+        sfar4[q] = dright_s[:, at_rows(far_base + q), :].reshape(block, length).astype(BF16)
+        copy(3, True, sfar4.at[q], far4.at[mine], q, mine).start()
+
+    for c in range(width):
+        dleft_s[c] = matmul(tri_s[c].astype(BF16), right_s[c].astype(BF16))
+
+    def grad_blocks(q):
+        return (
+            dleft_s[:, at_rows(q), :].reshape(block, length),
+            dright_s[:, at_rows(own_base + q), :].reshape(block, length),
+        )
+
+    @pl.loop(1, parts)
+    def _(t):
+        q = turn(t)
+        d_left, d_right = grad_blocks(q)
+        send4[q, pl.ds(0, block)] = d_left.astype(BF16)
+        send4[q, pl.ds(block, block)] = d_right.astype(BF16)
+        copy(3, False, send4.at[q], recv4.at[mine], q, mine).start()
+
+    d_left, d_right = grad_blocks(mine)
+    pos_buf[at_blocks(2 * mine, block), :] = d_left
+    pos_buf[at_blocks(2 * mine + 1, block), :] = d_right
+    gate_w, proj_w = gate_t.T.astype(BF16), proj_t.T.astype(BF16)
+
+    @pl.loop(1, parts)
+    def _(t):
+        s = turn(t)
+        copy(3, False, send4.at[s], recv4.at[s], s, s).wait_recv()
+        pos_buf[at_blocks(s, 2 * block), :] = recv4[s].astype(F32)
+
+    @pl.loop(0, parts)
+    def _(t):
+        s = turn(t)
+        copy(3, True, sfar4.at[s], far4.at[s], s, s).wait_recv()
+        pos_buf[at_blocks(2 * s + 1, block), :] += far4[s].astype(F32)
+
+    for i in range(ROWS):
+        grad = pos_buf[pl.ds(i, 2 * chans, stride=ROWS), :] * pair_mask[i : i + 1, :].astype(F32)
+        gate = gate_s[i]
+        d_proj = grad * gate
+        d_gate = d_proj * proj_s[i] * (1.0 - gate)
+        d_normed = (
+            matmul(gate_w, d_gate.astype(BF16))
+            + matmul(proj_w, d_proj.astype(BF16))
+            + matmul(w_gate[...], dpre_s[i])
+        )
+        normed = normed_s[i]
+        out[i] = inv_s[i] * (
+            d_normed
+            - jnp.mean(d_normed, axis=0, keepdims=True)
+            - normed * jnp.mean(d_normed * normed, axis=0, keepdims=True)
+        )
+
+    @pl.loop(0, parts)
+    def _(q):
+        copy(0, True, send1.at[q, pl.ds(block, block)], far1.at[q], q, q).wait_send()
+        copy(3, True, sfar4.at[q], far4.at[q], q, q).wait_send()
+
+    @pl.loop(1, parts)
+    def _(t):
+        q = turn(t)
+        copy(0, False, send1.at[q], recv1.at[q], q, q).wait_send()
+        copy(1, False, send2.at[q], recv2.at[q], q, q).wait_send()
+        copy(2, False, send3.at[q], recv3.at[q], q, q).wait_send()
+        copy(3, False, send4.at[q], recv4.at[q], q, q).wait_send()
+
+
+def fused_shards(n, *args):
+    rows, length, chans = args[0].shape
+    parts = n // 2
+    width = chans // parts
+    block = width * rows
+
+    def vmem(dtype, *shape):
+        return pltpu.VMEM(shape, dtype)
+
+    grad_t = pl.pallas_call(
+        functools.partial(fused_kernel, n),
+        out_shape=jax.ShapeDtypeStruct((rows, chans, length), F32),
+        in_specs=[pl.BlockSpec(memory_space=pltpu.HBM)] * 9,
+        out_specs=pl.BlockSpec(memory_space=pltpu.VMEM),
+        scratch_shapes=[pltpu.VMEM(x.shape, x.dtype) for x in args]
+        + [
+            vmem(F32, rows, chans, length),
+            vmem(BF16, rows, chans, length),
+            vmem(F32, rows, 1, length),
+            vmem(F32, rows, 2 * chans, length),
+            vmem(F32, rows, 2 * chans, length),
+            vmem(F32, rows, chans, length),
+            vmem(F32, rows, chans, length),
+            vmem(BF16, rows, chans, length),
+            vmem(F32, 2 * chans * rows, length),
+            vmem(F32, width, parts * rows, length),
+            vmem(F32, width, length, length),
+            vmem(F32, width, parts * rows, length),
+            vmem(F32, width, parts * rows, length),
+            vmem(F32, width, length, length),
+            vmem(BF16, parts, 2 * block, length),
+            vmem(BF16, parts, 2 * block, length),
+            vmem(BF16, parts, block, length),
+            vmem(BF16, parts, block, length),
+            vmem(BF16, parts, block, length),
+            vmem(BF16, parts, block, length),
+            vmem(BF16, parts, block, length),
+            vmem(BF16, parts, 2 * block, length),
+            vmem(BF16, parts, 2 * block, length),
+            vmem(BF16, parts, block, length),
+            vmem(BF16, parts, block, length),
+            pltpu.SemaphoreType.DMA((4, n)),
+            pltpu.SemaphoreType.DMA((4, n)),
+            pltpu.SemaphoreType.DMA((9,)),
+        ],
+        compiler_params=pltpu.CompilerParams(
+            collective_id=0, has_side_effects=True, vmem_limit_bytes=48 * 1024 * 1024
+        ),
+    )(*args)
+    return jnp.swapaxes(grad_t, 1, 2)
+
+
+def body_for(mesh):
+    n = mesh.shape["dap"]
+
+    def body(*args):
+        rows, length, chans = args[0].shape
+        fits = mesh.shape["ch"] == 1 and n == 16 and rows == ROWS
+        if fits and length == rows * n == chans:
+            return fused_shards(n, *args)
+        return shards(*args)
+
+    return body
+
+
 def solution(mesh):
     return jax.shard_map(
-        shards,
+        body_for(mesh),
         mesh=mesh,
         in_specs=(
             P(("grp", "dap"), None, None),

time: 209 us -> 54.5 us (0.26)
  waiting for transfers between devices: 149 us -> 0 us
  Pallas kernels: 0 us -> 45.7 us
  matrix products: 24 us -> 0 us
  between operations: 13.6 us -> 0.02 us
  local copies, waits for them, and re-layouts: 18.7 us -> 8.13 us
  other arithmetic: 2.32 us -> 0 us
    reduce_scatter x1 -> x0, waiting for transfers between devices: 96.6 us -> none  [shards(): lax.psum_scatter(jnp.einsum('ijc,ikc->jkc', d_tri, left, preferred_elemen...]
    all_gather x1 -> x0, waiting for transfers between devices: 52.5 us -> none  [shards(): right_all = lax.all_gather(right, 'dap', axis=0, tiled=True)]
    pallas_call x0 -> x1, Pallas kernels: none -> 45.7 us  [fused_shards(): pl.pallas_call(functools.partial(fused_kernel, n), out_shape=jax.ShapeDty...]
    dot_general x14 -> x0, matrix products: 24 us -> none  [the longest x11 11.7 us: matmul(): return jnp.dot(left, right, preferred_element_type=jnp.float32)]
    dot_general x2 -> x0, local copies, waits for them, and re-layouts: 9.6 us -> none  [the longest x1 9.36 us: shards(): jnp.einsum('ijc,ikc->jkc', d_tri, left, preferred_element_type=jnp.float32)]
    all_gather x1 -> x0, local copies, waits for them, and re-layouts: 6.73 us -> none  [shards(): right_all = lax.all_gather(right, 'dap', axis=0, tiled=True)]
    unnamed x19 -> x18, local copies, waits for them, and re-layouts: 1.16 us -> 7.13 us
  transfers between devices with their start and end apart: 2 -> 0, of which waited for: 2 -> 0; matrix products, arithmetic and copies ran while one was open for 4% -> 0% of each run, Pallas kernels for 0% -> 0%
where the time goes in v2:
time: 54.5 us; the launch traced here: 53.9 us
  Pallas kernels  45.7 us (84%)
  local copies, waits for them, and re-layouts  8.13 us (15%)
    pallas_call x1, Pallas kernels, fused_shards(): pl.pallas_call(functools.partial(fused_kernel, n), out_shape=jax.ShapeDty...  45.7 us
    unnamed x18, local copies, waits for them, and re-layouts  7.13 us

profile of v2, /device:TPU:0, one launch (start us, length us, event | category | flops | bytes accessed | tf_op | source)
XLA Modules:
  0.0 53.9 jit_solution(18193419200771999258)
XLA Ops:
  0.0 0.0 copy-start
  0.0 0.9 %copy-done = bf16[8,128,128]{2,1,0:T(8,128)(2,1)S(1)} copy-done((bf16[8,128,128]{2,1,0:T(8,128)(2,1)S(1)}, bf16[8,128,128]{2,1,0:T(8,128)(2,1)}, u32[]{:S(2)}) %copy-start) | copy-done | bytes 262168
  1.0 0.0 copy-start.1
  1.0 0.9 %copy-done.1 = bf16[8,128,128]{2,1,0:T(8,128)(2,1)S(1)} copy-done((bf16[8,128,128]{2,1,0:T(8,128)(2,1)S(1)}, bf16[8,128,128]{2,1,0:T(8,128)(2,1)}, u32[]{:S(2)}) %copy-start.1) | copy-done | bytes 262168
  1.9 0.0 copy-start.2
  1.9 0.8 %copy-done.2 = bf16[128,128]{1,0:T(8,128)(2,1)S(1)} copy-done((bf16[128,128]{1,0:T(8,128)(2,1)S(1)}, bf16[128,128]{1,0:T(8,128)(2,1)}, u32[]{:S(2)}) %copy-start.2) | copy-done | bytes 32792
  2.7 0.0 copy-start.3
  2.7 0.8 %copy-done.3 = bf16[128,128]{1,0:T(8,128)(2,1)S(1)} copy-done((bf16[128,128]{1,0:T(8,128)(2,1)S(1)}, bf16[128,128]{1,0:T(8,128)(2,1)}, u32[]{:S(2)}) %copy-start.3) | copy-done | bytes 32792
  3.4 0.0 copy-start.4
  3.4 0.8 %copy-done.4 = bf16[128,128]{1,0:T(8,128)(2,1)S(1)} copy-done((bf16[128,128]{1,0:T(8,128)(2,1)S(1)}, bf16[128,128]{1,0:T(8,128)(2,1)}, u32[]{:S(2)}) %copy-start.4) | copy-done | bytes 32792
  4.2 0.0 copy-start.5
  4.2 0.8 %copy-done.5 = bf16[128,128]{1,0:T(8,128)(2,1)S(1)} copy-done((bf16[128,128]{1,0:T(8,128)(2,1)S(1)}, bf16[128,128]{1,0:T(8,128)(2,1)}, u32[]{:S(2)}) %copy-start.5) | copy-done | bytes 32792
  4.9 0.0 copy-start.6
  4.9 0.8 %copy-done.6 = bf16[128,128]{1,0:T(8,128)(2,1)S(1)} copy-done((bf16[128,128]{1,0:T(8,128)(2,1)S(1)}, bf16[128,128]{1,0:T(8,128)(2,1)}, u32[]{:S(2)}) %copy-start.6) | copy-done | bytes 32792
  5.7 0.0 copy-start.7
  5.7 0.8 %copy-done.7 = bf16[128,128]{1,0:T(8,128)(2,1)S(1)} copy-done((bf16[128,128]{1,0:T(8,128)(2,1)S(1)}, bf16[128,128]{1,0:T(8,128)(2,1)}, u32[]{:S(2)}) %copy-start.7) | copy-done | bytes 32792
  6.5 0.0 copy-start.8
  6.5 0.7 %copy-done.8 = s32[8,128]{1,0:T(8,128)S(1)} copy-done((s32[8,128]{1,0:T(8,128)S(1)}, s32[8,128]{1,0:T(8,128)}, u32[]{:S(2)}) %copy-start.8) | copy-done | bytes 4120
  7.1 45.7 %shard_map.91 = f32[8,128,128]{2,1,0:T(8,128)S(1)} custom-call(bf16[8,128,128]{2,1,0:T(8,128)(2,1)S(1)} %copy-done, bf16[8,128,128]{2,1,0:T(8,128)(2,1)S(1)} %copy-done.1, s32[8,128]{1,0:T(8,128)S(1)} %copy-done.8, bf16[128,128]{1,0:T(8,128)(2,1)S(1)} %copy-done.2, bf16[128,128]{1,0:T(8,128)(2,1)S(1)} %copy-done.3, bf16[128,128]{1,0:T(8,128)(2,1)S(1)} %copy-done.4, ...), custom_call_target="tpu_custom_call" | custom-call | tf_op jit(solution)/shard_map/pallas_call | solution.py:344
  52.9 1.0 %copy.10 = f32[8,128,128]{2,1,0:T(8,128)} copy(f32[8,128,128]{1,2,0:T(8,128)S(1)} %bitcast.1) | data formatting | bytes 1048576 | tf_op jit(solution)/shard_map/transpose | solution.py:384
Async XLA Ops:
  0.0 0.9 %copy-start = (bf16[8,128,128]{2,1,0:T(8,128)(2,1)S(1)}, bf16[8,128,128]{2,1,0:T(8,128)(2,1)}, u32[]{:S(2)}) copy-start(bf16[8,128,128]{2,1,0:T(8,128)(2,1)} %refs_0_.1) | copy-start | bytes 786436
  1.0 0.9 %copy-start.1 = (bf16[8,128,128]{2,1,0:T(8,128)(2,1)S(1)}, bf16[8,128,128]{2,1,0:T(8,128)(2,1)}, u32[]{:S(2)}) copy-start(bf16[8,128,128]{2,1,0:T(8,128)(2,1)} %refs_1_.1) | copy-start | bytes 786436
  1.9 0.8 %copy-start.2 = (bf16[128,128]{1,0:T(8,128)(2,1)S(1)}, bf16[128,128]{1,0:T(8,128)(2,1)}, u32[]{:S(2)}) copy-start(bf16[128,128]{1,0:T(8,128)(2,1)} %refs_3_.1) | copy-start | bytes 98308
  2.7 0.8 %copy-start.3 = (bf16[128,128]{1,0:T(8,128)(2,1)S(1)}, bf16[128,128]{1,0:T(8,128)(2,1)}, u32[]{:S(2)}) copy-start(bf16[128,128]{1,0:T(8,128)(2,1)} %refs_4_.1) | copy-start | bytes 98308
  3.4 0.8 %copy-start.4 = (bf16[128,128]{1,0:T(8,128)(2,1)S(1)}, bf16[128,128]{1,0:T(8,128)(2,1)}, u32[]{:S(2)}) copy-start(bf16[128,128]{1,0:T(8,128)(2,1)} %refs_5_.1) | copy-start | bytes 98308
  4.2 0.8 %copy-start.5 = (bf16[128,128]{1,0:T(8,128)(2,1)S(1)}, bf16[128,128]{1,0:T(8,128)(2,1)}, u32[]{:S(2)}) copy-start(bf16[128,128]{1,0:T(8,128)(2,1)} %refs_6_.1) | copy-start | bytes 98308
  4.9 0.8 %copy-start.6 = (bf16[128,128]{1,0:T(8,128)(2,1)S(1)}, bf16[128,128]{1,0:T(8,128)(2,1)}, u32[]{:S(2)}) copy-start(bf16[128,128]{1,0:T(8,128)(2,1)} %refs_7_.1) | copy-start | bytes 98308
  5.7 0.8 %copy-start.7 = (bf16[128,128]{1,0:T(8,128)(2,1)S(1)}, bf16[128,128]{1,0:T(8,128)(2,1)}, u32[]{:S(2)}) copy-start(bf16[128,128]{1,0:T(8,128)(2,1)} %refs_8_.1) | copy-start | bytes 98308
  6.5 0.7 %copy-start.8 = (s32[8,128]{1,0:T(8,128)S(1)}, s32[8,128]{1,0:T(8,128)}, u32[]{:S(2)}) copy-start(s32[8,128]{1,0:T(8,128)} %refs_2_.1) | copy-start | bytes 12292

commit v3 on v2

--- a/solution.py
+++ b/solution.py
@@ -87,15 +87,19 @@
 
 
 def fused_kernel(n, *refs):
-    inputs, out, held, refs = refs[:9], refs[9], refs[10:19], refs[19:]
+    packed, out, held, refs = refs[0], refs[1], refs[2], refs[3:]
     (
         normed_s, nb_s, inv_s, gate_s, proj_s, og_s, dtrin_s, dpre_s, pos_buf, left_s, right_s, tri_s,
         dleft_s, dright_s, send1, recv1, far1, send2, recv2, send3, recv3, send4, recv4, sfar4, far4,
         send_sem, recv_sem, in_sem,
     ) = refs
-    pair, cotangent, pair_mask, w_a_gate, w_a_proj, w_b_gate, w_b_proj, w_gate, w_out = held
-    chans = w_out.shape[0]
-    length = pair.shape[1]
+    length = chans = held.shape[1]
+    size = ROWS * length
+    pair = [held.at[pl.ds(i * length, length)] for i in range(ROWS)]
+    cotangent = [held.at[pl.ds(size + i * length, length)] for i in range(ROWS)]
+    w_a_gate, w_a_proj, w_b_gate, w_b_proj, w_gate, w_out = [
+        held.at[pl.ds(2 * size + x * chans, chans)] for x in range(6)
+    ]
     parts = n // 2
     width = chans // parts
     block = width * ROWS
@@ -104,9 +108,8 @@
     own_base = me - mine
     far_base = parts - own_base
 
-    loads = [pltpu.make_async_copy(inputs[x], held[x], in_sem.at[x]) for x in range(9)]
-    for load in loads:
-        load.start()
+    load = pltpu.make_async_copy(packed, held, in_sem)
+    load.start()
 
     barrier = pltpu.get_barrier_semaphore()
 
@@ -142,13 +145,13 @@
     def grouped(values):
         return values.reshape(values.shape[0] // ROWS, ROWS, length)
 
-    for load in loads:
-        load.wait()
+    load.wait()
+    mask_f = held[pl.ds(2 * size + 6 * chans, 2 * ROWS), :].astype(F32)
     gate_t = interleaved(w_a_gate, w_b_gate, parts)
     proj_t = interleaved(w_a_proj, w_b_proj, parts)
     gate_tb, proj_tb = gate_t.astype(BF16), proj_t.astype(BF16)
     for i in range(ROWS):
-        x = pair[i].astype(F32).T
+        x = pair[i][...].astype(F32).T
         mu = jnp.mean(x, axis=0, keepdims=True)
         inv = lax.rsqrt(jnp.mean(x * x, axis=0, keepdims=True) - mu * mu + 1e-05)
         normed = (x - mu) * inv
@@ -164,7 +167,7 @@
             proj = matmul(proj_tb[rows], nb_s[i])
             gate_s[i, rows] = gate
             proj_s[i, rows] = proj
-            masked = pair_mask[i : i + 1, :].astype(F32)
+            masked = mask_f[i : i + 1, :]
             pos_buf[pl.ds(g * chans * ROWS + i, chans, stride=ROWS), :] = gate * proj * masked
         if g == 0:
             pl.semaphore_wait(barrier, n - 1)
@@ -182,7 +185,7 @@
     og_t = transposed(w_gate).astype(BF16)
     for i in range(ROWS):
         gate = jax.nn.sigmoid(matmul(og_t, nb_s[i]))
-        d_upd = cotangent[i].astype(F32).T * gate
+        d_upd = cotangent[i][...].astype(F32).T * gate
         dtrin_s[i] = matmul(w_out[...], d_upd.astype(BF16))
         og_s[i] = d_upd * (1.0 - gate)
 
@@ -302,7 +305,7 @@
         pos_buf[at_blocks(2 * s + 1, block), :] += far4[s].astype(F32)
 
     for i in range(ROWS):
-        grad = pos_buf[pl.ds(i, 2 * chans, stride=ROWS), :] * pair_mask[i : i + 1, :].astype(F32)
+        grad = pos_buf[pl.ds(i, 2 * chans, stride=ROWS), :] * mask_f[i : i + 1, :]
         gate = gate_s[i]
         d_proj = grad * gate
         d_gate = d_proj * proj_s[i] * (1.0 - gate)
@@ -338,16 +341,22 @@
     width = chans // parts
     block = width * rows
 
+    pair, cotangent, pair_mask = args[:3]
+    packed = jnp.concatenate(
+        [pair.reshape(-1, chans), cotangent.reshape(-1, chans), *args[3:]]
+        + [pair_mask.astype(BF16), jnp.zeros((ROWS, length), BF16)]
+    )
+
     def vmem(dtype, *shape):
         return pltpu.VMEM(shape, dtype)
 
     grad_t = pl.pallas_call(
         functools.partial(fused_kernel, n),
         out_shape=jax.ShapeDtypeStruct((rows, chans, length), F32),
-        in_specs=[pl.BlockSpec(memory_space=pltpu.HBM)] * 9,
+        in_specs=[pl.BlockSpec(memory_space=pltpu.HBM)],
         out_specs=pl.BlockSpec(memory_space=pltpu.VMEM),
-        scratch_shapes=[pltpu.VMEM(x.shape, x.dtype) for x in args]
-        + [
+        scratch_shapes=[
+            vmem(BF16, *packed.shape),
             vmem(F32, rows, chans, length),
             vmem(BF16, rows, chans, length),
             vmem(F32, rows, 1, length),
@@ -375,12 +384,12 @@
             vmem(BF16, parts, block, length),
             pltpu.SemaphoreType.DMA((4, n)),
             pltpu.SemaphoreType.DMA((4, n)),
-            pltpu.SemaphoreType.DMA((9,)),
+            pltpu.SemaphoreType.DMA,
         ],
         compiler_params=pltpu.CompilerParams(
             collective_id=0, has_side_effects=True, vmem_limit_bytes=48 * 1024 * 1024
         ),
-    )(*args)
+    )(packed)
     return jnp.swapaxes(grad_t, 1, 2)
 
 

time: 54.5 us -> 53.5 us (0.982)
  local copies, waits for them, and re-layouts: 8.13 us -> 7.24 us
    unnamed x18 -> x24, local copies, waits for them, and re-layouts: 7.13 us -> 6.24 us
where the time goes in v3:
time: 53.5 us; the launch traced here: 53 us
  Pallas kernels  45.7 us (85%)
  local copies, waits for them, and re-layouts  7.24 us (14%)
    pallas_call x1, Pallas kernels, fused_shards(): pl.pallas_call(functools.partial(fused_kernel, n), out_shape=jax.ShapeDty...  45.7 us
    unnamed x24, local copies, waits for them, and re-layouts  6.24 us

profile of v3, /device:TPU:0, one launch (start us, length us, event | category | flops | bytes accessed | tf_op | source)
XLA Modules:
  0.0 53.0 jit_solution(7308098484147620370)
XLA Ops:
  0.0 0.0 copy-start
  0.0 1.0 %constant_dynamic-update-slice_fusion.9 = bf16[2832,128]{1,0:T(8,128)(2,1)S(1)} fusion(bf16[1024,128]{1,0:T(8,128)(2,1)} %bitcast.4), kind=kLoop, calls=%fused_computation.9 | loop fusion | bytes 524288
  1.0 0.0 copy-done
  1.0 0.0 copy-start.1
  1.1 0.7 %copy-done.1 = bf16[128,128]{1,0:T(8,128)(2,1)S(1)} copy-done((bf16[128,128]{1,0:T(8,128)(2,1)S(1)}, bf16[128,128]{1,0:T(8,128)(2,1)}, u32[]{:S(2)}) %copy-start.1) | copy-done | bytes 32792
  1.8 0.0 copy-start.2
  1.8 0.7 %copy-done.2 = bf16[128,128]{1,0:T(8,128)(2,1)S(1)} copy-done((bf16[128,128]{1,0:T(8,128)(2,1)S(1)}, bf16[128,128]{1,0:T(8,128)(2,1)}, u32[]{:S(2)}) %copy-start.2) | copy-done | bytes 32792
  2.5 0.0 copy-start.3
  2.6 0.7 %copy-done.3 = bf16[128,128]{1,0:T(8,128)(2,1)S(1)} copy-done((bf16[128,128]{1,0:T(8,128)(2,1)S(1)}, bf16[128,128]{1,0:T(8,128)(2,1)}, u32[]{:S(2)}) %copy-start.3) | copy-done | bytes 32792
  3.3 0.0 copy-start.4
  3.3 0.7 %copy-done.4 = bf16[128,128]{1,0:T(8,128)(2,1)S(1)} copy-done((bf16[128,128]{1,0:T(8,128)(2,1)S(1)}, bf16[128,128]{1,0:T(8,128)(2,1)}, u32[]{:S(2)}) %copy-start.4) | copy-done | bytes 32792
  4.1 0.0 copy-start.5
  4.1 0.7 %copy-done.5 = bf16[128,128]{1,0:T(8,128)(2,1)S(1)} copy-done((bf16[128,128]{1,0:T(8,128)(2,1)S(1)}, bf16[128,128]{1,0:T(8,128)(2,1)}, u32[]{:S(2)}) %copy-start.5) | copy-done | bytes 32792
  4.8 0.0 copy-start.6
  4.8 0.7 %copy-done.6 = bf16[128,128]{1,0:T(8,128)(2,1)S(1)} copy-done((bf16[128,128]{1,0:T(8,128)(2,1)S(1)}, bf16[128,128]{1,0:T(8,128)(2,1)}, u32[]{:S(2)}) %copy-start.6) | copy-done | bytes 32792
  5.6 0.0 copy-start.7
  5.6 0.7 %copy-done.7 = s32[8,128]{1,0:T(8,128)S(1)} copy-done((s32[8,128]{1,0:T(8,128)S(1)}, s32[8,128]{1,0:T(8,128)}, u32[]{:S(2)}) %copy-start.7) | copy-done | bytes 4120
  6.3 45.7 %shard_map.91 = f32[8,128,128]{2,1,0:T(8,128)S(1)} custom-call(bf16[2832,128]{1,0:T(8,128)(2,1)S(1)} %constant_dynamic-update-slice_fusion.refs_0_), custom_call_target="tpu_custom_call" | custom-call | tf_op jit(solution)/shard_map/pallas_call | solution.py:353
  52.0 1.0 %copy.10 = f32[8,128,128]{2,1,0:T(8,128)} copy(f32[8,128,128]{1,2,0:T(8,128)S(1)} %bitcast.3) | data formatting | bytes 1048576 | tf_op jit(solution)/shard_map/transpose | solution.py:393
  (9 shorter events, 0.1 us)
Async XLA Ops:
  0.0 1.0 %copy-start = (bf16[8,128,128]{2,1,0:T(8,128)(2,1)S(1)}, bf16[8,128,128]{2,1,0:T(8,128)(2,1)}, u32[]{:S(2)}) copy-start(bf16[8,128,128]{2,1,0:T(8,128)(2,1)} %param.10) | copy-start | bytes 786436
  1.0 0.8 %copy-start.1 = (bf16[128,128]{1,0:T(8,128)(2,1)S(1)}, bf16[128,128]{1,0:T(8,128)(2,1)}, u32[]{:S(2)}) copy-start(bf16[128,128]{1,0:T(8,128)(2,1)} %param.12) | copy-start | bytes 98308
  1.8 0.8 %copy-start.2 = (bf16[128,128]{1,0:T(8,128)(2,1)S(1)}, bf16[128,128]{1,0:T(8,128)(2,1)}, u32[]{:S(2)}) copy-start(bf16[128,128]{1,0:T(8,128)(2,1)} %param.13) | copy-start | bytes 98308
  2.5 0.8 %copy-start.3 = (bf16[128,128]{1,0:T(8,128)(2,1)S(1)}, bf16[128,128]{1,0:T(8,128)(2,1)}, u32[]{:S(2)}) copy-start(bf16[128,128]{1,0:T(8,128)(2,1)} %param.14) | copy-start | bytes 98308
  3.3 0.8 %copy-start.4 = (bf16[128,128]{1,0:T(8,128)(2,1)S(1)}, bf16[128,128]{1,0:T(8,128)(2,1)}, u32[]{:S(2)}) copy-start(bf16[128,128]{1,0:T(8,128)(2,1)} %param.15) | copy-start | bytes 98308
  4.1 0.8 %copy-start.5 = (bf16[128,128]{1,0:T(8,128)(2,1)S(1)}, bf16[128,128]{1,0:T(8,128)(2,1)}, u32[]{:S(2)}) copy-start(bf16[128,128]{1,0:T(8,128)(2,1)} %param.16) | copy-start | bytes 98308
  4.8 0.8 %copy-start.6 = (bf16[128,128]{1,0:T(8,128)(2,1)S(1)}, bf16[128,128]{1,0:T(8,128)(2,1)}, u32[]{:S(2)}) copy-start(bf16[128,128]{1,0:T(8,128)(2,1)} %param.17) | copy-start | bytes 98308
  5.6 0.7 %copy-start.7 = (s32[8,128]{1,0:T(8,128)S(1)}, s32[8,128]{1,0:T(8,128)}, u32[]{:S(2)}) copy-start(s32[8,128]{1,0:T(8,128)} %param.11) | copy-start | bytes 12292
